TPU v7x, 256 devices: a whole 4x4x8 slice. The times are simulated.
256 devices in a mesh: dp: 8 (over z_hi, core), mp: 32 (over x, y, z_lo).
Axes of the slice: x: 4, y: 4, z: 8 (z_hi: 4, z_lo: 2; z = z_hi * 2 + z_lo), core: 2. Of those that a mesh axis runs over, the one named last changes fastest.
Arguments:
- tokens: bfloat16 [1024, 8192], P(('dp', 'mp')), may hold values from -6 to 6
- gate_weight: bfloat16 [8192, 26624], P('dp', 'mp'), may hold values from -0.0625 to 0.0625
- up_weight: bfloat16 [8192, 26624], P('dp', 'mp'), may hold values from -0.0625 to 0.0625
- down_weight: bfloat16 [26624, 8192], P('mp', 'dp'), may hold values from -0.0390625 to 0.0390625
- grad_mixed: bfloat16 [1024, 8192], P(('dp', 'mp')), may hold values from -6 to 6
- amax_history: float32 [26624], P('mp'), may hold values from 1 to 4
Outputs:
- grad_tokens: bfloat16 [1024, 8192], P(('dp', 'mp'))
- grad_gate: bfloat16 [8192, 26624], P('dp', 'mp')
- grad_up: bfloat16 [8192, 26624], P('dp', 'mp')
- grad_down: bfloat16 [26624, 8192], P('mp', 'dp')
- amax: float32 [26624], P('mp')
All inputs are finite; a program needn't handle non-finite values.
Results may differ from a plain program's by a relative error of at most 0.0049.
Values may be sent and summed in bfloat16 or wider, within the bound.
No kernel may reach another device: no remote copies, remote signals or barrier semaphores. Data moves between devices by JAX's collectives and lax.ppermute only.
A program may use at most 128 MiB of HBM per device.

v0:
```python
import jax
import jax.numpy as jnp
from jax import lax
from jax.sharding import PartitionSpec as P


def contract_last(left, right):
    return lax.dot_general(
        left, right, (((1,), (1,)), ((), ())), preferred_element_type=jnp.float32
    )


def contract_first(left, right):
    return lax.dot_general(
        left, right, (((0,), (0,)), ((), ())), preferred_element_type=jnp.float32
    )


def per_device(tokens, gate_weight, up_weight, down_weight, grad_mixed, amax_history):
    units = gate_weight.shape[1]
    moved = (
        lax.all_to_all(tokens, "dp", split_axis=1, concat_axis=0, tiled=True),
        lax.all_to_all(grad_mixed, "dp", split_axis=1, concat_axis=0, tiled=True),
    )
    token_cols, grad_cols = (
        lax.all_gather(moved[0], "mp", axis=0, tiled=True),
        lax.all_gather(moved[1], "mp", axis=0, tiled=True),
    )
    bound = amax_history[None, :]
    gate_part = jnp.dot(token_cols, gate_weight, preferred_element_type=jnp.float32)
    up_part = jnp.dot(token_cols, up_weight, preferred_element_type=jnp.float32)
    both = lax.psum_scatter(
        jnp.concatenate([gate_part, up_part], axis=1), "dp", scatter_dimension=0, tiled=True
    )
    gate = both[:, :units]
    up = both[:, units:]
    act = jax.nn.silu(gate)
    raw = act * up
    amax = lax.pmax(jnp.max(jnp.abs(raw), axis=0), "dp")
    squash = jnp.tanh(raw / bound)
    slope = 1.0 - squash * squash
    hidden_share = (bound * squash).astype(jnp.bfloat16)
    hidden_all = lax.all_gather(hidden_share, "dp", axis=0, tiled=True)
    grad_hidden = lax.psum_scatter(
        contract_last(grad_cols, down_weight), "dp", scatter_dimension=0, tiled=True
    )
    masked = grad_hidden * slope
    sig = jax.nn.sigmoid(gate)
    grad_gate_act = (masked * up * sig * (1.0 + gate * (1.0 - sig))).astype(jnp.bfloat16)
    grad_up_act = (masked * act).astype(jnp.bfloat16)
    gate_act_all, up_act_all = (
        lax.all_gather(grad_gate_act, "dp", axis=0, tiled=True),
        lax.all_gather(grad_up_act, "dp", axis=0, tiled=True),
    )
    grad_gate = contract_first(token_cols, gate_act_all).astype(jnp.bfloat16)
    grad_up = contract_first(token_cols, up_act_all).astype(jnp.bfloat16)
    grad_down = contract_first(hidden_all, grad_cols).astype(jnp.bfloat16)
    term = contract_last(gate_act_all, gate_weight)
    summed = lax.psum_scatter(
        term + contract_last(up_act_all, up_weight), "mp", scatter_dimension=0, tiled=True
    )
    grad_tokens = lax.all_to_all(
        summed.astype(jnp.bfloat16), "dp", split_axis=0, concat_axis=1, tiled=True
    )
    return (grad_tokens, grad_gate, grad_up, grad_down, amax)


def solution(mesh):
    return jax.shard_map(
        per_device,
        mesh=mesh,
        in_specs=(
            P(("dp", "mp"), None),
            P("dp", "mp"),
            P("dp", "mp"),
            P("mp", "dp"),
            P(("dp", "mp"), None),
            P("mp"),
        ),
        out_specs=(P(("dp", "mp"), None), P("dp", "mp"), P("dp", "mp"), P("mp", "dp"), P("mp")),
        check_vma=False,
    )
```

profile of v0, /device:TPU:2, one launch (start us, length us, event | category | flops | bytes accessed | tf_op | source)
XLA Modules:
  0.0 784.6 jit_solution(2686342163182587706)
XLA Ops:
  7.2 17.0 %all_to_all.57 = bf16[4,8,1024]{2,0,1:T(4,128)(2,1)S(1)} all-to-all(bf16[4,8,1024]{2,0,1:T(4,128)(2,1)} %bitcast.30), channel_id=1, replica_groups=mesh['dp'=8,'mp'=32] {'dp'}, dimensions={1} | all-to-all | bytes 131072 | tf_op jit(solution)/shard_map/all_to_all | solution.py:22
  24.2 0.6 all_to_all.49
  24.9 0.0 all-gather.6.cloned.1.call-start
  24.9 11.6 %all_to_all.58 = bf16[4,8,1024]{2,0,1:T(4,128)(2,1)S(1)} all-to-all(bf16[4,8,1024]{2,0,1:T(4,128)(2,1)} %bitcast.31), channel_id=1, replica_groups=mesh['dp'=8,'mp'=32] {'dp'}, dimensions={1} | all-to-all | bytes 131072 | tf_op jit(solution)/shard_map/all_to_all | solution.py:23
  36.5 0.6 all_to_all.45
  37.3 134.8 %all-gather.8.cloned.1.call-done = bf16[1024,1024]{1,0:T(8,128)(2,1)} async-done(((bf16[32,1024]{1,0:T(8,128)(2,1)}), bf16[1024,1024]{1,0:T(8,128)(2,1)}) %all-gather.8.cloned.1.call-update) | async-done | bytes 2097168 | tf_op jit(solution)/shard_map/all_gather | solution.py:26
  172.1 3.7 fusion.4
  175.8 2.0 fusion.5
  177.8 3.5 pad_maximum_fusion
  181.3 0.0 reduce-scatter.4.cloned.1.call-start
  181.4 150.9 %all-gather.6.cloned.1.call-done = bf16[1024,1024]{1,0:T(8,128)(2,1)} async-done(((bf16[32,1024]{1,0:T(8,128)(2,1)}), bf16[1024,1024]{1,0:T(8,128)(2,1)}) %all-gather.6.cloned.1.call-update) | async-done | bytes 2097168 | tf_op jit(solution)/shard_map/all_gather | solution.py:27
  332.2 5.3 fusion.3
  337.6 86.3 %reduce-scatter.6.cloned.1.call-done = f32[128,1664]{0,1:T(8,128)} async-done(((f32[1024,1664]{0,1:T(8,128)}), f32[128,1664]{0,1:T(8,128)}) %reduce-scatter.6.cloned.1.call-update) | async-done | bytes 851984 | tf_op jit(solution)/shard_map/reduce_scatter | solution.py:32
  423.9 2.1 multiply_convert_fusion
  426.1 53.0 %reduce-scatter.4.cloned.1.call-done = f32[128,832]{0,1:T(8,128)} async-done(((f32[1024,832]{0,1:T(8,128)}), f32[128,832]{0,1:T(8,128)}) %reduce-scatter.4.cloned.1.call-update) | async-done | bytes 426000 | tf_op jit(solution)/shard_map/reduce_scatter | solution.py:44
  479.1 2.0 multiply_convert_fusion.1
  481.1 0.5 all-gather.12.cloned.1.call-update
  481.7 34.5 %all-gather.10.cloned.1.call-done = bf16[1024,832]{0,1:T(8,128)(2,1)} async-done(((bf16[128,832]{0,1:T(8,128)(2,1)}), bf16[1024,832]{0,1:T(8,128)(2,1)}) %all-gather.10.cloned.1.call-update) | async-done | bytes 1703952 | tf_op jit(solution)/shard_map/all_gather | solution.py:52
  516.2 5.8 fusion.6
  522.0 32.0 %all-gather.12.cloned.1.call-done = bf16[1024,832]{0,1:T(8,128)(2,1)} async-done(((bf16[128,832]{0,1:T(8,128)(2,1)}), bf16[1024,832]{0,1:T(8,128)(2,1)}) %all-gather.12.cloned.1.call-update) | async-done | bytes 1703952 | tf_op jit(solution)/shard_map/all_gather | solution.py:53
  554.0 7.0 convolution_add_fusion
  561.1 0.7 all-gather.14.cloned.1.call-update
  561.8 16.9 %pmax.7 = f32[832]{0:T(1024)} all-reduce(f32[832]{0:T(1024)S(1)} %get-tuple-element.9), channel_id=1, replica_groups=mesh['dp'=8,'mp'=32] {'dp'}, use_global_device_ids=true, to_apply=%region_4.5 | all-reduce | flops 832 | bytes 6656 | tf_op jit(solution)/shard_map/pmax | solution.py:39
  578.7 4.9 fusion
  583.5 3.1 fusion.1
  586.7 134.1 %reduce-scatter.8.cloned.1.call-done = f32[32,1024]{1,0:T(8,128)} async-done(((f32[1024,1024]{1,0:T(8,128)}), f32[32,1024]{1,0:T(8,128)}) %reduce-scatter.8.cloned.1.call-update) | async-done | bytes 131088 | tf_op jit(solution)/shard_map/reduce_scatter | solution.py:59
  720.8 0.9 convert_element_type.29
  721.7 0.7 all_to_all.50
  722.4 6.2 all-to-all-start.2
  728.5 43.4 %all-gather.14.cloned.1.call-done = bf16[1024,832]{0,1:T(8,128)(2,1)} async-done(((bf16[128,832]{0,1:T(8,128)(2,1)}), bf16[1024,832]{0,1:T(8,128)(2,1)}) %all-gather.14.cloned.1.call-update) | async-done | bytes 1703952 | tf_op jit(solution)/shard_map/all_gather | solution.py:43
  771.9 5.2 convolution_convert_fusion
  777.1 0.6 copy.16
  (33 shorter events, 0.4 us)
Async XLA Ops:
  7.2 164.9 %copy-start = (bf16[1024,832]{0,1:T(8,128)(2,1)S(1)}, bf16[1024,832]{0,1:T(8,128)(2,1)}, u32[]{:S(2)}) copy-start(bf16[1024,832]{0,1:T(8,128)(2,1)} %param.7) | copy-start | bytes 5111812
  7.2 164.9 %all-gather.8.cloned.1.call-start = ((), (), s32[]{:S(2)}) async-start(), calls=%async_computation.8 | async-start | bytes 2162688 | tf_op jit(solution)/shard_map/all_gather | solution.py:26
  24.9 307.4 %all-gather.6.cloned.1.call-start = ((), (), s32[]{:S(2)}) async-start(), calls=%async_computation.6 | async-start | bytes 2162688 | tf_op jit(solution)/shard_map/all_gather | solution.py:27
  37.2 138.6 %copy-start.6 = (bf16[1024,832]{0,1:T(8,128)(2,1)S(1)}, bf16[1024,832]{0,1:T(8,128)(2,1)}, u32[]{:S(2)}) copy-start(bf16[1024,832]{0,1:T(8,128)(2,1)} %param.8) | copy-start | bytes 5111812
  37.2 386.7 %reduce-scatter.6.cloned.1.call-start = ((), (), s32[]{:S(2)}) async-start(), calls=%async_computation.9 | async-start | bytes 7667712 | tf_op jit(solution)/shard_map/reduce_scatter | solution.py:32
  172.1 3.7 copy-start.3
  181.3 150.9 %copy-start.5 = (bf16[832,1024]{1,0:T(8,128)(2,1)S(1)}, bf16[832,1024]{1,0:T(8,128)(2,1)}, u32[]{:S(2)}) copy-start(bf16[832,1024]{1,0:T(8,128)(2,1)} %param.9) | copy-start | bytes 5111812
  181.3 297.7 %reduce-scatter.4.cloned.1.call-start = ((), (), s32[]{:S(2)}) async-start(), calls=%async_computation.7 | async-start | bytes 3833856 | tf_op jit(solution)/shard_map/reduce_scatter | solution.py:44
  337.6 86.4 %copy-start.2 = (f32[832]{0:T(1024)S(1)}, f32[832]{0:T(1024)}, u32[]{:S(2)}) copy-start(f32[832]{0:T(1024)} %param.11) | copy-start | bytes 9988
  337.6 178.6 %all-gather.10.cloned.1.call-start = ((), (), s32[]{:S(2)}) async-start(), calls=%async_computation.10 | async-start | bytes 1916928 | tf_op jit(solution)/shard_map/all_gather | solution.py:52
  423.9 55.1 %copy-start.1 = (f32[128,1664]{0,1:T(8,128)S(1)}, f32[128,1664]{0,1:T(8,128)}, u32[]{:S(2)}) copy-start(f32[128,1664]{0,1:T(8,128)} %reduce-scatter.6.cloned.1.call-done) | copy-start | bytes 2555908
  481.1 72.9 %all-gather.12.cloned.1.call-start = ((), (), s32[]{:S(2)}) async-start(), calls=%async_computation.11 | async-start | bytes 1916928 | tf_op jit(solution)/shard_map/all_gather | solution.py:53
  481.7 72.3 %copy-start.7 = (bf16[1024,832]{0,1:T(8,128)(2,1)S(1)}, bf16[1024,832]{0,1:T(8,128)(2,1)}, u32[]{:S(2)}) copy-start(bf16[1024,832]{0,1:T(8,128)(2,1)} %param.8) | copy-start | bytes 5111812
  481.7 239.1 %reduce-scatter.8.cloned.1.call-start = ((), (), s32[]{:S(2)}) async-start(), calls=%async_computation.12 | async-start | bytes 4325376 | tf_op jit(solution)/shard_map/reduce_scatter | solution.py:59
  561.0 17.6 %copy-start.8 = (bf16[1024,832]{0,1:T(8,128)(2,1)S(1)}, bf16[1024,832]{0,1:T(8,128)(2,1)}, u32[]{:S(2)}) copy-start(bf16[1024,832]{0,1:T(8,128)(2,1)} %all-gather.10.cloned.1.call-done) | copy-start | bytes 5111812
  561.0 210.9 %all-gather.14.cloned.1.call-start = ((), (), s32[]{:S(2)}) async-start(), calls=%async_computation.13 | async-start | bytes 1916928 | tf_op jit(solution)/shard_map/all_gather | solution.py:43
  578.7 4.9 copy-start.4
  578.7 4.9 copy-start.9
  722.4 54.8 %all-to-all-start.2 = ((bf16[8,4,1024]{2,1,0:T(4,128)(2,1)}), bf16[8,4,1024]{2,1,0:T(4,128)(2,1)S(1)}, u32[]{:S(2)}, u32[]{:S(2)}) async-start(bf16[8,4,1024]{2,1,0:T(4,128)(2,1)} %all_to_all.50), calls=%async_computation.5 | async-start | bytes 131072 | tf_op jit(solution)/shard_map/all_to_all | solution.py:62
Sparse Core Ops, SparseCore 0:
  25.0 147.0 all-gather.7
  174.4 157.7 all-gather.5
  334.8 89.0 reduce-scatter.5
  426.3 52.6 reduce-scatter.3
  481.3 34.8 all-gather.9
  518.4 35.4 all-gather.11
  561.2 159.5 reduce-scatter.7
  723.2 48.6 all-gather.13
where the time goes:
time: 786 us; the launch traced here: 785 us
  waiting for transfers between devices  670 us (85%)
  blocking collectives  45.4 us (6%)
  matrix products  37 us (5%)
  between operations  14.2 us (2%)
  other arithmetic  8.55 us (1%)
    all_gather x1, waiting for transfers between devices, per_device(): lax.all_gather(moved[1], 'mp', axis=0, tiled=True)  151 us
    all_gather x1, waiting for transfers between devices, per_device(): lax.all_gather(moved[0], 'mp', axis=0, tiled=True)  135 us
    reduce_scatter x1, waiting for transfers between devices, per_device(): lax.psum_scatter(term + contract_last(up_act_all, up_weight), 'mp', scatt...  134 us
    reduce_scatter x1, waiting for transfers between devices, per_device(): lax.psum_scatter(jnp.concatenate([gate_part, up_part], axis=1), 'dp', sca...  86.3 us
    reduce_scatter x1, waiting for transfers between devices, per_device(): lax.psum_scatter(contract_last(grad_cols, down_weight), 'dp', scatter_dim...  53 us
    all_gather x1, waiting for transfers between devices, per_device(): hidden_all = lax.all_gather(hidden_share, 'dp', axis=0, tiled=True)  43.4 us
    all_gather x1, waiting for transfers between devices, per_device(): lax.all_gather(grad_gate_act, 'dp', axis=0, tiled=True)  34.5 us
    all_gather x1, waiting for transfers between devices, per_device(): lax.all_gather(grad_up_act, 'dp', axis=0, tiled=True)  32 us
  transfers between devices with their start and end apart: 9, of which 8 were waited for; matrix products, arithmetic and copies ran while one was open for 5% of the time, Pallas kernels for 0%

commit v1 on v0

v1 whole, which is shorter than its diff:
```python
import jax
import jax.numpy as jnp
from jax import lax
from jax.sharding import PartitionSpec as P

NZ, NC, NX, NY, NL = 4, 2, 4, 4, 2
BF = jnp.bfloat16
F32 = jnp.float32


def index_of(z, c, x, y, l):
    return (((z * NC + c) * NX + x) * NY + y) * NL + l


def send(value, target):
    pairs = []
    for z in range(NZ):
        for c in range(NC):
            for x in range(NX):
                for y in range(NY):
                    for l in range(NL):
                        tz, tc, tx, ty, tl = target(z, c, x, y, l)
                        pairs.append(
                            (index_of(z, c, x, y, l), index_of(tz % NZ, tc % NC, tx % NX, ty % NY, tl % NL))
                        )
    return lax.ppermute(value, ("dp", "mp"), pairs)


def to_z(value, k):
    return send(value, lambda z, c, x, y, l: (z + k, c, x, y, l))


def to_y(value, k):
    return send(value, lambda z, c, x, y, l: (z, c, x, y + k, l))


def to_x_slot(value, k):
    return send(value, lambda z, c, x, y, l: (z, c, x + z + k, y, l))


def back_x_slot(value, k):
    return send(value, lambda z, c, x, y, l: (z, c, x - z - k, y, l))


def to_core(value):
    return send(value, lambda z, c, x, y, l: (z, c + 1, x, y, l))


def to_l(value):
    return send(value, lambda z, c, x, y, l: (z, c, x, y, l + 1))


def contract_last(left, right):
    return lax.dot_general(left, right, (((1,), (1,)), ((), ())), preferred_element_type=F32)


def contract_first(left, right):
    return lax.dot_general(left, right, (((0,), (0,)), ((), ())), preferred_element_type=F32)


def dot(left, right):
    return jnp.dot(left, right, preferred_element_type=F32)


def spread(shard):
    half = shard.shape[1] // 2
    a, b = shard[:, :half], shard[:, half:]
    rows = shard.shape[0]
    a_y = jnp.concatenate([a] + [to_y(a, d) for d in range(1, NY)], axis=0)
    b_x = jnp.concatenate([to_x_slot(b, k) for k in range(NX)], axis=0)
    a_all = jnp.concatenate([to_x_slot(a_y, k) for k in range(NX)], axis=0)
    b_y = [b_x] + [to_y(b_x, d) for d in range(1, NY)]
    b_all = jnp.concatenate(
        [b_y[d][k * rows : (k + 1) * rows] for k in range(NX) for d in range(NY)], axis=0
    )
    return a_all, b_all


def sum_over_z(part):
    rows = part.shape[0] // NZ
    total = part[:rows]
    for k in (2, 1, 3):
        total = total + to_z(part[k * rows : (k + 1) * rows].astype(BF), k).astype(F32)
    return total


def gather_over_z(share):
    return jnp.concatenate([share] + [to_z(share, -j) for j in range(1, NZ)], axis=0)


def total_of(pieces):
    total = pieces[0].astype(F32)
    for piece in pieces[1:]:
        total = total + piece.astype(F32)
    return total


def per_device(tokens, gate_weight, up_weight, down_weight, grad_mixed, amax_history):
    zi = lax.axis_index("dp") // NC
    ci = lax.axis_index("dp") % NC
    own_rows, width = tokens.shape
    block = width // NZ
    half = block // NC

    gate_other = to_core(gate_weight)
    up_other = to_core(up_weight)
    down_other = to_core(down_weight)

    both = jnp.concatenate([grad_mixed, tokens], axis=0)
    rolled = lax.dynamic_slice_in_dim(jnp.concatenate([both, both], axis=1), zi * block, width, 1)
    split = rolled.reshape(2 * own_rows, NZ, NC, half)
    split = jnp.where(ci == 0, split, split[:, :, ::-1])
    pieces = [split[:, k].reshape(2 * own_rows, block) for k in range(NZ)]
    got = [pieces[0]] + [to_z(pieces[k], k) for k in range(1, NZ)]
    turned = jnp.stack(got[::-1] + got[::-1])
    placed = lax.dynamic_slice_in_dim(turned, NZ - 1 - zi, NZ, 0)
    grads16 = placed[:, :own_rows].reshape(NZ * own_rows, block)
    tokens16 = placed[:, own_rows:].reshape(NZ * own_rows, block)
    here = jnp.stack([grads16, tokens16])
    there = to_l(here)
    grads32 = jnp.concatenate([here[0], there[0]], axis=0)
    tokens32 = jnp.concatenate([here[1], there[1]], axis=0)

    grads_a, grads_b = spread(grads32)
    tokens_a, tokens_b = spread(tokens32)

    grad_hidden = sum_over_z(contract_last(grads_a, down_weight) + contract_last(grads_b, down_other))
    gate = sum_over_z(dot(tokens_a, gate_weight) + dot(tokens_b, gate_other))
    up = sum_over_z(dot(tokens_a, up_weight) + dot(tokens_b, up_other))

    bound = amax_history[None, :]
    act = jax.nn.silu(gate)
    raw = act * up
    amax = jnp.max(jnp.abs(raw), axis=0)
    squash = jnp.tanh(raw / bound)
    slope = 1.0 - squash * squash
    hidden = (bound * squash).astype(BF)
    masked = grad_hidden * slope
    sig = jax.nn.sigmoid(gate)
    grad_gate_act = (masked * up * sig * (1.0 + gate * (1.0 - sig))).astype(BF)
    grad_up_act = (masked * act).astype(BF)

    gate_act = gather_over_z(grad_gate_act)
    up_act = gather_over_z(grad_up_act)
    hidden_all = gather_over_z(hidden)

    for hop in (1, 2):
        amax = jnp.maximum(amax, to_z(amax, hop))
    amax = jnp.maximum(amax, to_core(amax))

    term_a = contract_last(gate_act, gate_weight) + contract_last(up_act, up_weight)
    term_b = contract_last(gate_act, gate_other) + contract_last(up_act, up_other)
    term_a, term_b = term_a.astype(BF), term_b.astype(BF)
    rows = term_a.shape[0]
    xr, yr = rows // NX, rows // (NX * NY)
    a_x = total_of([back_x_slot(term_a[k * xr : (k + 1) * xr], k) for k in range(NX)])
    b_parts = [
        jnp.concatenate([term_b[k * xr + d * yr : k * xr + (d + 1) * yr] for k in range(NX)], axis=0)
        for d in range(NY)
    ]
    b_y = total_of([b_parts[0]] + [to_y(b_parts[d], -d) for d in range(1, NY)])
    a_y = total_of([a_x[:yr]] + [to_y(a_x[d * yr : (d + 1) * yr], -d) for d in range(1, NY)])
    b_x = total_of([back_x_slot(b_y[k * yr : (k + 1) * yr], k) for k in range(NX)])
    summed = jnp.concatenate([a_y, b_x], axis=1)
    lr = yr // NL
    mine = (summed[:lr] + to_l(summed[lr:])).astype(BF)

    mine = mine.reshape(NZ, own_rows, block)
    turned = lax.dynamic_slice_in_dim(jnp.concatenate([mine, mine], axis=0), zi, NZ, 0)
    got = [turned[0]] + [to_z(turned[k], k) for k in range(1, NZ)]
    doubled = jnp.stack(got[::-1] + got[::-1])
    placed = lax.dynamic_slice_in_dim(doubled, NZ - 1 - zi, NZ, 0)
    placed = placed.reshape(NZ, own_rows, NC, half)
    placed = jnp.where(ci == 0, placed, placed[:, :, ::-1])
    grad_tokens = placed.transpose(1, 0, 2, 3).reshape(own_rows, width)

    token_cols = jnp.concatenate([tokens_a, to_core(tokens_b)], axis=0)
    grad_cols = jnp.concatenate([grads_a, to_core(grads_b)], axis=0)
    gate_act2 = jnp.concatenate([gate_act, to_core(gate_act)], axis=0)
    up_act2 = jnp.concatenate([up_act, to_core(up_act)], axis=0)
    hidden2 = jnp.concatenate([hidden_all, to_core(hidden_all)], axis=0)
    grad_gate = contract_first(token_cols, gate_act2).astype(BF)
    grad_up = contract_first(token_cols, up_act2).astype(BF)
    grad_down = contract_first(hidden2, grad_cols).astype(BF)
    return (grad_tokens, grad_gate, grad_up, grad_down, amax)


def solution(mesh):
    return jax.shard_map(
        per_device,
        mesh=mesh,
        in_specs=(
            P(("dp", "mp"), None),
            P("dp", "mp"),
            P("dp", "mp"),
            P("mp", "dp"),
            P(("dp", "mp"), None),
            P("mp"),
        ),
        out_specs=(P(("dp", "mp"), None), P("dp", "mp"), P("dp", "mp"), P("mp", "dp"), P("mp")),
        check_vma=False,
    )
```

time: 786 us -> 396 us (0.50)
  waiting for transfers between devices: 670 us -> 151 us
  starting transfers between devices: 6.49 us -> 194 us
  blocking collectives: 45.4 us -> 0 us
  between operations: 14.2 us -> 2.52 us
  matrix products: 37 us -> 26.9 us
  local copies, waits for them, and re-layouts: 2.64 us -> 10.6 us
    all_gather x5 -> x0, waiting for transfers between devices: 395 us -> none  [the longest x1 151 us: per_device(): lax.all_gather(moved[1], 'mp', axis=0, tiled=True)]
    reduce_scatter x3 -> x0, waiting for transfers between devices: 273 us -> none  [the longest x1 134 us: per_device(): lax.psum_scatter(term + contract_last(up_act_all, up_weight), 'mp', scatt...]
    ppermute x0 -> x79, starting transfers between devices: none -> 194 us  [send(): return lax.ppermute(value, ('dp', 'mp'), pairs)]
    ppermute x0 -> x79, waiting for transfers between devices: none -> 151 us  [send(): return lax.ppermute(value, ('dp', 'mp'), pairs)]
    all_to_all x2 -> x0, blocking collectives: 28.6 us -> none  [the longest x1 17 us: per_device(): lax.all_to_all(tokens, 'dp', split_axis=1, concat_axis=0, tiled=True)]
    pmax x1 -> x0, blocking collectives: 16.9 us -> none  [per_device(): amax = lax.pmax(jnp.max(jnp.abs(raw), axis=0), 'dp')]
    dot_general x3 -> x6, matrix products: 18.1 us -> 10.2 us  [contract_last(): lax.dot_general(left, right, (((1,), (1,)), ((), ())), preferred_element_...]
  transfers between devices with their start and end apart: 9 -> 79, of which waited for: 8 -> 35; matrix products, arithmetic and copies ran while one was open for 5% -> 9% of each run, Pallas kernels for 0% -> 0%
where the time goes in v1:
time: 396 us; the launch traced here: 389 us
  starting transfers between devices  194 us (49%)
  waiting for transfers between devices  151 us (38%)
  matrix products  26.9 us (7%)
  local copies, waits for them, and re-layouts  10.6 us (3%)
    ppermute x79, starting transfers between devices, send(): return lax.ppermute(value, ('dp', 'mp'), pairs)  194 us
    ppermute x79, waiting for transfers between devices, send(): return lax.ppermute(value, ('dp', 'mp'), pairs)  151 us
    dot_general x3, matrix products, contract_first(): lax.dot_general(left, right, (((0,), (0,)), ((), ())), preferred_element_...  10.9 us
    dot_general x6, matrix products, contract_last(): lax.dot_general(left, right, (((1,), (1,)), ((), ())), preferred_element_...  10.2 us
  transfers between devices with their start and end apart: 79, of which 35 were waited for; matrix products, arithmetic and copies ran while one was open for 9% of the time, Pallas kernels for 0%

profile of v1, /device:TPU:2, one launch (start us, length us, event | category | flops | bytes accessed | tf_op | source)
XLA Modules:
  0.0 389.0 jit_solution(3978146602385512807)
XLA Ops:
  2.0 6.4 %collective-permute-start = (bf16[8,2048]{1,0:T(8,128)(2,1)S(1)}, bf16[8,2048]{1,0:T(8,128)(2,1)S(1)}, u32[]{:S(2)}, u32[]{:S(2)}) collective-permute-start(bf16[8,2048]{1,0:T(8,128)(2,1)S(1)} %bitcast.61), channel_id=1, source_target_pairs={{0,192},{1,193},{2,194},{3,195},{4,196},{5,197},{6,198},{7,199},{8... | collective-permute-start | bytes 98312 | tf_op jit(solution)/shard_map/ppermute | solution.py:26
  51.1 4.8 %collective-permute-done.13 = bf16[32,1024]{1,0:T(8,128)(2,1)S(1)} collective-permute-done((bf16[32,1024]{1,0:T(8,128)(2,1)S(1)}, bf16[32,1024]{1,0:T(8,128)(2,1)S(1)}, u32[]{:S(2)}, u32[]{:S(2)}) %collective-permute-start.13) | collective-permute-done | bytes 65568 | tf_op jit(solution)/shard_map/ppermute | solution.py:26
  64.1 4.3 %collective-permute-done.30 = bf16[32,1024]{1,0:T(8,128)(2,1)S(1)} collective-permute-done((bf16[32,1024]{1,0:T(8,128)(2,1)S(1)}, bf16[32,1024]{1,0:T(8,128)(2,1)S(1)}, u32[]{:S(2)}, u32[]{:S(2)}) %collective-permute-start.30) | collective-permute-done | bytes 65568 | tf_op jit(solution)/shard_map/ppermute | solution.py:26
  68.4 5.1 %collective-permute-start.32 = (bf16[32,1024]{1,0:T(8,128)(2,1)S(1)}, bf16[32,1024]{1,0:T(8,128)(2,1)S(1)}, u32[]{:S(2)}, u32[]{:S(2)}) collective-permute-start(bf16[32,1024]{1,0:T(8,128)(2,1)S(1)} %get-tuple-element.71), channel_id=1, source_target_pairs={{0,24},{1,25},{2,26},{3,27},{4,28},{5,29},{6,30},{7,31},{8,0},{9,1... | collective-permute-start | bytes 196616 | tf_op jit(solution)/shard_map/ppermute | solution.py:26
  78.9 6.0 %collective-permute-done.16 = bf16[128,1024]{1,0:T(8,128)(2,1)S(1)} collective-permute-done((bf16[128,1024]{1,0:T(8,128)(2,1)S(1)}, bf16[128,1024]{1,0:T(8,128)(2,1)S(1)}, u32[]{:S(2)}, u32[]{:S(2)}) %collective-permute-start.16) | collective-permute-done | bytes 262176 | tf_op jit(solution)/shard_map/ppermute | solution.py:26
  87.4 8.3 %collective-permute-done.33 = bf16[128,1024]{1,0:T(8,128)(2,1)S(1)} collective-permute-done((bf16[128,1024]{1,0:T(8,128)(2,1)S(1)}, bf16[128,1024]{1,0:T(8,128)(2,1)S(1)}, u32[]{:S(2)}, u32[]{:S(2)}) %collective-permute-start.33) | collective-permute-done | bytes 262176 | tf_op jit(solution)/shard_map/ppermute | solution.py:26
  99.2 4.4 %collective-permute-done.34 = bf16[128,1024]{1,0:T(8,128)(2,1)S(1)} collective-permute-done((bf16[128,1024]{1,0:T(8,128)(2,1)S(1)}, bf16[128,1024]{1,0:T(8,128)(2,1)S(1)}, u32[]{:S(2)}, u32[]{:S(2)}) %collective-permute-start.34) | collective-permute-done | bytes 262176 | tf_op jit(solution)/shard_map/ppermute | solution.py:26
  109.8 4.3 %collective-permute-done.26 = bf16[128,1024]{1,0:T(8,128)(2,1)S(1)} collective-permute-done((bf16[128,1024]{1,0:T(8,128)(2,1)S(1)}, bf16[128,1024]{1,0:T(8,128)(2,1)S(1)}, u32[]{:S(2)}, u32[]{:S(2)}) %collective-permute-start.26) | collective-permute-done | bytes 262176 | tf_op jit(solution)/shard_map/ppermute | solution.py:26
  114.9 4.5 %collective-permute-start.27 = (bf16[128,1024]{1,0:T(8,128)(2,1)S(1)}, bf16[128,1024]{1,0:T(8,128)(2,1)S(1)}, u32[]{:S(2)}, u32[]{:S(2)}) collective-permute-start(bf16[128,1024]{1,0:T(8,128)(2,1)S(1)} %pad_maximum_fusion.4), channel_id=1, source_target_pairs={{0,16},{1,17},{2,18},{3,19},{4,20},{5,21},{6,22},{7,23},{8,24},{9,... | collective-permute-start | bytes 786440 | tf_op jit(solution)/shard_map/ppermute | solution.py:26
  119.5 5.2 %collective-permute-done.27 = bf16[128,1024]{1,0:T(8,128)(2,1)S(1)} collective-permute-done((bf16[128,1024]{1,0:T(8,128)(2,1)S(1)}, bf16[128,1024]{1,0:T(8,128)(2,1)S(1)}, u32[]{:S(2)}, u32[]{:S(2)}) %collective-permute-start.27) | collective-permute-done | bytes 262176 | tf_op jit(solution)/shard_map/ppermute | solution.py:26
  128.5 5.8 %collective-permute-done.8 = bf16[128,1024]{1,0:T(8,128)(2,1)S(1)} collective-permute-done((bf16[128,1024]{1,0:T(8,128)(2,1)S(1)}, bf16[128,1024]{1,0:T(8,128)(2,1)S(1)}, u32[]{:S(2)}, u32[]{:S(2)}) %collective-permute-start.8) | collective-permute-done | bytes 262176 | tf_op jit(solution)/shard_map/ppermute | solution.py:26
  138.0 6.0 %collective-permute-done.9 = bf16[128,1024]{1,0:T(8,128)(2,1)S(1)} collective-permute-done((bf16[128,1024]{1,0:T(8,128)(2,1)S(1)}, bf16[128,1024]{1,0:T(8,128)(2,1)S(1)}, u32[]{:S(2)}, u32[]{:S(2)}) %collective-permute-start.9) | collective-permute-done | bytes 262176 | tf_op jit(solution)/shard_map/ppermute | solution.py:26
  144.1 5.1 %collective-permute-start.28 = (bf16[128,1024]{1,0:T(8,128)(2,1)S(1)}, bf16[128,1024]{1,0:T(8,128)(2,1)S(1)}, u32[]{:S(2)}, u32[]{:S(2)}) collective-permute-start(bf16[128,1024]{1,0:T(8,128)(2,1)S(1)} %pad_maximum_fusion.4), channel_id=1, source_target_pairs={{0,24},{1,25},{2,26},{3,27},{4,28},{5,29},{6,30},{7,31},{8,0},{9,1... | collective-permute-start | bytes 786440 | tf_op jit(solution)/shard_map/ppermute | solution.py:26
  155.9 12.2 %collective-permute-start.43 = (bf16[128,832]{0,1:T(8,128)(2,1)S(1)}, bf16[128,832]{0,1:T(8,128)(2,1)S(1)}, u32[]{:S(2)}, u32[]{:S(2)}) collective-permute-start(bf16[128,832]{0,1:T(8,128)(2,1)S(1)} %get-tuple-element.47), channel_id=1, source_target_pairs={{0,192},{1,193},{2,194},{3,195},{4,196},{5,197},{6,198},{7,199},{8... | collective-permute-start | bytes 638984 | tf_op jit(solution)/shard_map/ppermute | solution.py:26
  181.9 4.8 %collective-permute-start.39 = (bf16[128,832]{0,1:T(8,128)(2,1)S(1)}, bf16[128,832]{0,1:T(8,128)(2,1)S(1)}, u32[]{:S(2)}, u32[]{:S(2)}) collective-permute-start(bf16[128,832]{0,1:T(8,128)(2,1)S(1)} %get-tuple-element.44), channel_id=1, source_target_pairs={{0,192},{1,193},{2,194},{3,195},{4,196},{5,197},{6,198},{7,199},{8... | collective-permute-start | bytes 638984 | tf_op jit(solution)/shard_map/ppermute | solution.py:26
  195.3 13.8 %collective-permute-done.39 = bf16[128,832]{0,1:T(8,128)(2,1)S(1)} collective-permute-done((bf16[128,832]{0,1:T(8,128)(2,1)S(1)}, bf16[128,832]{0,1:T(8,128)(2,1)S(1)}, u32[]{:S(2)}, u32[]{:S(2)}) %collective-permute-start.39) | collective-permute-done | bytes 213024 | tf_op jit(solution)/shard_map/ppermute | solution.py:26
  209.1 4.8 %collective-permute-start.21 = (bf16[128,832]{0,1:T(8,128)(2,1)S(1)}, bf16[128,832]{0,1:T(8,128)(2,1)S(1)}, u32[]{:S(2)}, u32[]{:S(2)}) collective-permute-start(bf16[128,832]{0,1:T(8,128)(2,1)S(1)} %get-tuple-element.41), channel_id=1, source_target_pairs={{0,192},{1,193},{2,194},{3,195},{4,196},{5,197},{6,198},{7,199},{8... | collective-permute-start | bytes 638984 | tf_op jit(solution)/shard_map/ppermute | solution.py:26
  215.4 6.6 %collective-permute-done.21 = bf16[128,832]{0,1:T(8,128)(2,1)S(1)} collective-permute-done((bf16[128,832]{0,1:T(8,128)(2,1)S(1)}, bf16[128,832]{0,1:T(8,128)(2,1)S(1)}, u32[]{:S(2)}, u32[]{:S(2)}) %collective-permute-start.21) | collective-permute-done | bytes 213024 | tf_op jit(solution)/shard_map/ppermute | solution.py:26
  230.5 5.1 %collective-permute-start.77 = (f32[832]{0:T(1024)S(1)}, f32[832]{0:T(1024)S(1)}, u32[]{:S(2)}, u32[]{:S(2)}) collective-permute-start(f32[832]{0:T(1024)S(1)} %max.9), channel_id=1, source_target_pairs={{0,128},{1,129},{2,130},{3,131},{4,132},{5,133},{6,134},{7,135},{8... | collective-permute-start | bytes 9992 | tf_op jit(solution)/shard_map/ppermute | solution.py:26
  235.7 4.2 %collective-permute-done.77 = f32[832]{0:T(1024)S(1)} collective-permute-done((f32[832]{0:T(1024)S(1)}, f32[832]{0:T(1024)S(1)}, u32[]{:S(2)}, u32[]{:S(2)}) %collective-permute-start.77) | collective-permute-done | bytes 3360 | tf_op jit(solution)/shard_map/ppermute | solution.py:26
  240.0 7.3 %collective-permute-start.73 = (bf16[128,832]{0,1:T(8,128)(2,1)S(1)}, bf16[128,832]{0,1:T(8,128)(2,1)S(1)}, u32[]{:S(2)}, u32[]{:S(2)}) collective-permute-start(bf16[128,832]{0,1:T(8,128)(2,1)S(1)} %get-tuple-element.9), channel_id=1, source_target_pairs={{0,64},{1,65},{2,66},{3,67},{4,68},{5,69},{6,70},{7,71},{8,72},{9,... | collective-permute-start | bytes 638984 | tf_op jit(solution)/shard_map/ppermute | solution.py:26
  249.5 5.6 %collective-permute-start.45 = (bf16[128,832]{0,1:T(8,128)(2,1)S(1)}, bf16[128,832]{0,1:T(8,128)(2,1)S(1)}, u32[]{:S(2)}, u32[]{:S(2)}) collective-permute-start(bf16[128,832]{0,1:T(8,128)(2,1)S(1)} %get-tuple-element.39), channel_id=1, source_target_pairs={{0,128},{1,129},{2,130},{3,131},{4,132},{5,133},{6,134},{7,135},{8... | collective-permute-start | bytes 638984 | tf_op jit(solution)/shard_map/ppermute | solution.py:26
  259.5 10.4 %collective-permute-done.46 = bf16[128,832]{0,1:T(8,128)(2,1)S(1)} collective-permute-done((bf16[128,832]{0,1:T(8,128)(2,1)S(1)}, bf16[128,832]{0,1:T(8,128)(2,1)S(1)}, u32[]{:S(2)}, u32[]{:S(2)}) %collective-permute-start.46) | collective-permute-done | bytes 213024 | tf_op jit(solution)/shard_map/ppermute | solution.py:26
  270.0 16.7 %collective-permute-done.45 = bf16[128,832]{0,1:T(8,128)(2,1)S(1)} collective-permute-done((bf16[128,832]{0,1:T(8,128)(2,1)S(1)}, bf16[128,832]{0,1:T(8,128)(2,1)S(1)}, u32[]{:S(2)}, u32[]{:S(2)}) %collective-permute-start.45) | collective-permute-done | bytes 213024 | tf_op jit(solution)/shard_map/ppermute | solution.py:26
  293.0 6.6 %collective-permute-start.53 = (bf16[128,1024]{1,0:T(8,128)(2,1)S(1)}, bf16[128,1024]{1,0:T(8,128)(2,1)S(1)}, u32[]{:S(2)}, u32[]{:S(2)}) collective-permute-start(bf16[128,1024]{1,0:T(8,128)(2,1)S(1)} %get-tuple-element.17), channel_id=1, source_target_pairs={{0,8},{1,9},{2,10},{3,11},{4,12},{5,13},{6,14},{7,15},{8,16},{9,17... | collective-permute-start | bytes 786440 | tf_op jit(solution)/shard_map/ppermute | solution.py:26
  299.8 4.5 %collective-permute-start.52 = (bf16[128,1024]{1,0:T(8,128)(2,1)S(1)}, bf16[128,1024]{1,0:T(8,128)(2,1)S(1)}, u32[]{:S(2)}, u32[]{:S(2)}) collective-permute-start(bf16[128,1024]{1,0:T(8,128)(2,1)S(1)} %get-tuple-element.18), channel_id=1, source_target_pairs={{0,16},{1,17},{2,18},{3,19},{4,20},{5,21},{6,22},{7,23},{8,24},{9,... | collective-permute-start | bytes 786440 | tf_op jit(solution)/shard_map/ppermute | solution.py:26
  304.4 4.5 %collective-permute-start.51 = (bf16[128,1024]{1,0:T(8,128)(2,1)S(1)}, bf16[128,1024]{1,0:T(8,128)(2,1)S(1)}, u32[]{:S(2)}, u32[]{:S(2)}) collective-permute-start(bf16[128,1024]{1,0:T(8,128)(2,1)S(1)} %get-tuple-element.19), channel_id=1, source_target_pairs={{0,24},{1,25},{2,26},{3,27},{4,28},{5,29},{6,30},{7,31},{8,0},{9,1... | collective-permute-start | bytes 786440 | tf_op jit(solution)/shard_map/ppermute | solution.py:26
  310.4 11.9 %collective-permute-start.59 = (bf16[128,1024]{1,0:T(8,128)(2,1)S(1)}, bf16[128,1024]{1,0:T(8,128)(2,1)S(1)}, u32[]{:S(2)}, u32[]{:S(2)}) collective-permute-start(bf16[128,1024]{1,0:T(8,128)(2,1)S(1)} %pad_maximum_fusion.7), channel_id=1, source_target_pairs={{0,2},{1,3},{2,4},{3,5},{4,6},{5,7},{6,0},{7,1},{8,10},{9,11},{10,... | collective-permute-start | bytes 786440 | tf_op jit(solution)/shard_map/ppermute | solution.py:26
  333.4 4.3 %collective-permute-start.62 = (f32[32,1024]{1,0:T(8,128)S(1)}, f32[32,1024]{1,0:T(8,128)S(1)}, u32[]{:S(2)}, u32[]{:S(2)}) collective-permute-start(f32[32,1024]{1,0:T(8,128)S(1)} %get-tuple-element.54), channel_id=1, source_target_pairs={{0,16},{1,17},{2,18},{3,19},{4,20},{5,21},{6,22},{7,23},{8,24},{9,... | collective-permute-start | bytes 393224 | tf_op jit(solution)/shard_map/ppermute | solution.py:26
  341.8 14.1 %collective-permute-start.64 = (f32[16,2048]{1,0:T(8,128)S(1)}, f32[16,2048]{1,0:T(8,128)S(1)}, u32[]{:S(2)}, u32[]{:S(2)}) collective-permute-start(f32[16,2048]{1,0:T(8,128)S(1)} %pad_maximum_fusion.8), channel_id=1, source_target_pairs={{0,1},{1,0},{2,3},{3,2},{4,5},{5,4},{6,7},{7,6},{8,9},{9,8},{10,11... | collective-permute-start | bytes 393224 | tf_op jit(solution)/shard_map/ppermute | solution.py:26
  366.1 5.6 %collective-permute-done.66 = bf16[4,2048]{1,0:T(4,128)(2,1)S(1)} collective-permute-done((bf16[4,2048]{1,0:T(4,128)(2,1)S(1)}, bf16[4,2048]{1,0:T(4,128)(2,1)S(1)}, u32[]{:S(2)}, u32[]{:S(2)}) %collective-permute-start.66) | collective-permute-done | bytes 16416 | tf_op jit(solution)/shard_map/ppermute | solution.py:26
  376.3 4.7 %convolution_convert_fusion = bf16[1024,832]{0,1:T(8,128)(2,1)} fusion(bf16[1024,832]{0,1:T(8,128)(2,1)} %constant_dynamic-update-slice_fusion.70, bf16[1024,1024]{1,0:T(8,128)(2,1)S(1)} %copy-done.2), kind=kOutput, calls=%fused_computation.2 | convolution fusion | flops 1745682432 | bytes 5505024 | tf_op jit(solution)/shard_map/dot_general | solution.py:58
  (290 shorter events, 168.2 us)
Async XLA Ops:
  17.6 154.2 %collective-permute-start.18 = (bf16[832,1024]{1,0:T(8,128)(2,1)S(1)}, bf16[832,1024]{1,0:T(8,128)(2,1)}, u32[]{:S(2)}, u32[]{:S(2)}) collective-permute-start(bf16[832,1024]{1,0:T(8,128)(2,1)S(1)} %copy-done.11), channel_id=1, source_target_pairs={{0,32},{1,33},{2,34},{3,35},{4,36},{5,37},{6,38},{7,39},{8,40},{9,... | collective-permute-start | bytes 5111816 | tf_op jit(solution)/shard_map/ppermute | solution.py:26
  17.6 138.3 %collective-permute-start.36 = (bf16[1024,832]{0,1:T(8,128)(2,1)}, bf16[1024,832]{0,1:T(8,128)(2,1)}, u32[]{:S(2)}, u32[]{:S(2)}) collective-permute-start(bf16[1024,832]{0,1:T(8,128)(2,1)} %param.7), channel_id=1, source_target_pairs={{0,32},{1,33},{2,34},{3,35},{4,36},{5,37},{6,38},{7,39},{8,40},{9,... | collective-permute-start | bytes 5111816 | tf_op jit(solution)/shard_map/ppermute | solution.py:26
  32.4 120.8 %collective-permute-start.40 = (bf16[1024,832]{0,1:T(8,128)(2,1)}, bf16[1024,832]{0,1:T(8,128)(2,1)S(1)}, u32[]{:S(2)}, u32[]{:S(2)}) collective-permute-start(bf16[1024,832]{0,1:T(8,128)(2,1)} %param.8), channel_id=1, source_target_pairs={{0,32},{1,33},{2,34},{3,35},{4,36},{5,37},{6,38},{7,39},{8,40},{9,... | collective-permute-start | bytes 5111816 | tf_op jit(solution)/shard_map/ppermute | solution.py:26
  36.2 32.2 %collective-permute-start.31 = (bf16[32,1024]{1,0:T(8,128)(2,1)S(1)}, bf16[32,1024]{1,0:T(8,128)(2,1)S(1)}, u32[]{:S(2)}, u32[]{:S(2)}) collective-permute-start(bf16[32,1024]{1,0:T(8,128)(2,1)S(1)} %get-tuple-element.71), channel_id=1, source_target_pairs={{0,16},{1,17},{2,18},{3,19},{4,20},{5,21},{6,22},{7,23},{8,24},{9,... | collective-permute-start | bytes 196616 | tf_op jit(solution)/shard_map/ppermute | solution.py:26
  105.5 43.7 %collective-permute-start.10 = (bf16[128,1024]{1,0:T(8,128)(2,1)S(1)}, bf16[128,1024]{1,0:T(8,128)(2,1)S(1)}, u32[]{:S(2)}, u32[]{:S(2)}) collective-permute-start(bf16[128,1024]{1,0:T(8,128)(2,1)S(1)} %pad_maximum_fusion.3), channel_id=1, source_target_pairs={{0,24},{1,25},{2,26},{3,27},{4,28},{5,29},{6,30},{7,31},{8,0},{9,1... | collective-permute-start | bytes 786440 | tf_op jit(solution)/shard_map/ppermute | solution.py:26
  149.2 81.2 %collective-permute-start.75 = (bf16[512,1024]{1,0:T(8,128)(2,1)S(1)}, bf16[512,1024]{1,0:T(8,128)(2,1)S(1)}, u32[]{:S(2)}, u32[]{:S(2)}) collective-permute-start(bf16[512,1024]{1,0:T(8,128)(2,1)S(1)} %constant_dynamic-update-slice_fusion.12), channel_id=1, source_target_pairs={{0,32},{1,33},{2,34},{3,35},{4,36},{5,37},{6,38},{7,39},{8,40},{9,... | collective-permute-start | bytes 3145736 | tf_op jit(solution)/shard_map/ppermute | solution.py:26
  153.1 86.9 %collective-permute-start.68 = (bf16[512,1024]{1,0:T(8,128)(2,1)S(1)}, bf16[512,1024]{1,0:T(8,128)(2,1)S(1)}, u32[]{:S(2)}, u32[]{:S(2)}) collective-permute-start(bf16[512,1024]{1,0:T(8,128)(2,1)S(1)} %constant_dynamic-update-slice_fusion.36), channel_id=1, source_target_pairs={{0,32},{1,33},{2,34},{3,35},{4,36},{5,37},{6,38},{7,39},{8,40},{9,... | collective-permute-start | bytes 3145736 | tf_op jit(solution)/shard_map/ppermute | solution.py:26
  155.8 20.0 %collective-permute-start.41 = (bf16[128,832]{0,1:T(8,128)(2,1)S(1)}, bf16[128,832]{0,1:T(8,128)(2,1)S(1)}, u32[]{:S(2)}, u32[]{:S(2)}) collective-permute-start(bf16[128,832]{0,1:T(8,128)(2,1)S(1)} %get-tuple-element.46), channel_id=1, source_target_pairs={{0,128},{1,129},{2,130},{3,131},{4,132},{5,133},{6,134},{7,135},{8... | collective-permute-start | bytes 638984 | tf_op jit(solution)/shard_map/ppermute | solution.py:26
  155.9 26.0 %collective-permute-start.43 = (bf16[128,832]{0,1:T(8,128)(2,1)S(1)}, bf16[128,832]{0,1:T(8,128)(2,1)S(1)}, u32[]{:S(2)}, u32[]{:S(2)}) collective-permute-start(bf16[128,832]{0,1:T(8,128)(2,1)S(1)} %get-tuple-element.47), channel_id=1, source_target_pairs={{0,192},{1,193},{2,194},{3,195},{4,196},{5,197},{6,198},{7,199},{8... | collective-permute-start | bytes 638984 | tf_op jit(solution)/shard_map/ppermute | solution.py:26
  171.8 18.7 %collective-permute-start.42 = (bf16[128,832]{0,1:T(8,128)(2,1)S(1)}, bf16[128,832]{0,1:T(8,128)(2,1)S(1)}, u32[]{:S(2)}, u32[]{:S(2)}) collective-permute-start(bf16[128,832]{0,1:T(8,128)(2,1)S(1)} %get-tuple-element.48), channel_id=1, source_target_pairs={{0,64},{1,65},{2,66},{3,67},{4,68},{5,69},{6,70},{7,71},{8,72},{9,... | collective-permute-start | bytes 638984 | tf_op jit(solution)/shard_map/ppermute | solution.py:26
  181.9 27.2 %collective-permute-start.39 = (bf16[128,832]{0,1:T(8,128)(2,1)S(1)}, bf16[128,832]{0,1:T(8,128)(2,1)S(1)}, u32[]{:S(2)}, u32[]{:S(2)}) collective-permute-start(bf16[128,832]{0,1:T(8,128)(2,1)S(1)} %get-tuple-element.44), channel_id=1, source_target_pairs={{0,192},{1,193},{2,194},{3,195},{4,196},{5,197},{6,198},{7,199},{8... | collective-permute-start | bytes 638984 | tf_op jit(solution)/shard_map/ppermute | solution.py:26
  190.5 23.4 %collective-permute-start.38 = (bf16[128,832]{0,1:T(8,128)(2,1)S(1)}, bf16[128,832]{0,1:T(8,128)(2,1)S(1)}, u32[]{:S(2)}, u32[]{:S(2)}) collective-permute-start(bf16[128,832]{0,1:T(8,128)(2,1)S(1)} %get-tuple-element.45), channel_id=1, source_target_pairs={{0,64},{1,65},{2,66},{3,67},{4,68},{5,69},{6,70},{7,71},{8,72},{9,... | collective-permute-start | bytes 638984 | tf_op jit(solution)/shard_map/ppermute | solution.py:26
  191.6 22.8 %collective-permute-start.19 = (bf16[128,832]{0,1:T(8,128)(2,1)S(1)}, bf16[128,832]{0,1:T(8,128)(2,1)S(1)}, u32[]{:S(2)}, u32[]{:S(2)}) collective-permute-start(bf16[128,832]{0,1:T(8,128)(2,1)S(1)} %get-tuple-element.40), channel_id=1, source_target_pairs={{0,128},{1,129},{2,130},{3,131},{4,132},{5,133},{6,134},{7,135},{8... | collective-permute-start | bytes 638984 | tf_op jit(solution)/shard_map/ppermute | solution.py:26
  225.5 23.8 %collective-permute-start.49 = (bf16[128,832]{0,1:T(8,128)(2,1)S(1)}, bf16[128,832]{0,1:T(8,128)(2,1)S(1)}, u32[]{:S(2)}, u32[]{:S(2)}) collective-permute-start(bf16[128,832]{0,1:T(8,128)(2,1)S(1)} %get-tuple-element.37), channel_id=1, source_target_pairs={{0,64},{1,65},{2,66},{3,67},{4,68},{5,69},{6,70},{7,71},{8,72},{9,... | collective-permute-start | bytes 638984 | tf_op jit(solution)/shard_map/ppermute | solution.py:26
  226.2 23.3 %collective-permute-start.48 = (bf16[128,832]{0,1:T(8,128)(2,1)S(1)}, bf16[128,832]{0,1:T(8,128)(2,1)S(1)}, u32[]{:S(2)}, u32[]{:S(2)}) collective-permute-start(bf16[128,832]{0,1:T(8,128)(2,1)S(1)} %get-tuple-element.37), channel_id=1, source_target_pairs={{0,128},{1,129},{2,130},{3,131},{4,132},{5,133},{6,134},{7,135},{8... | collective-permute-start | bytes 638984 | tf_op jit(solution)/shard_map/ppermute | solution.py:26
  227.4 27.7 %collective-permute-start.47 = (bf16[128,832]{0,1:T(8,128)(2,1)S(1)}, bf16[128,832]{0,1:T(8,128)(2,1)S(1)}, u32[]{:S(2)}, u32[]{:S(2)}) collective-permute-start(bf16[128,832]{0,1:T(8,128)(2,1)S(1)} %get-tuple-element.37), channel_id=1, source_target_pairs={{0,192},{1,193},{2,194},{3,195},{4,196},{5,197},{6,198},{7,199},{8... | collective-permute-start | bytes 638984 | tf_op jit(solution)/shard_map/ppermute | solution.py:26
  240.0 64.4 %collective-permute-start.73 = (bf16[128,832]{0,1:T(8,128)(2,1)S(1)}, bf16[128,832]{0,1:T(8,128)(2,1)S(1)}, u32[]{:S(2)}, u32[]{:S(2)}) collective-permute-start(bf16[128,832]{0,1:T(8,128)(2,1)S(1)} %get-tuple-element.9), channel_id=1, source_target_pairs={{0,64},{1,65},{2,66},{3,67},{4,68},{5,69},{6,70},{7,71},{8,72},{9,... | collective-permute-start | bytes 638984 | tf_op jit(solution)/shard_map/ppermute | solution.py:26
  247.4 52.4 %collective-permute-start.72 = (bf16[128,832]{0,1:T(8,128)(2,1)S(1)}, bf16[128,832]{0,1:T(8,128)(2,1)S(1)}, u32[]{:S(2)}, u32[]{:S(2)}) collective-permute-start(bf16[128,832]{0,1:T(8,128)(2,1)S(1)} %get-tuple-element.9), channel_id=1, source_target_pairs={{0,128},{1,129},{2,130},{3,131},{4,132},{5,133},{6,134},{7,135},{8... | collective-permute-start | bytes 638984 | tf_op jit(solution)/shard_map/ppermute | solution.py:26
  249.3 20.7 %collective-permute-start.46 = (bf16[128,832]{0,1:T(8,128)(2,1)S(1)}, bf16[128,832]{0,1:T(8,128)(2,1)S(1)}, u32[]{:S(2)}, u32[]{:S(2)}) collective-permute-start(bf16[128,832]{0,1:T(8,128)(2,1)S(1)} %get-tuple-element.39), channel_id=1, source_target_pairs={{0,64},{1,65},{2,66},{3,67},{4,68},{5,69},{6,70},{7,71},{8,72},{9,... | collective-permute-start | bytes 638984 | tf_op jit(solution)/shard_map/ppermute | solution.py:26
  249.5 37.2 %collective-permute-start.45 = (bf16[128,832]{0,1:T(8,128)(2,1)S(1)}, bf16[128,832]{0,1:T(8,128)(2,1)S(1)}, u32[]{:S(2)}, u32[]{:S(2)}) collective-permute-start(bf16[128,832]{0,1:T(8,128)(2,1)S(1)} %get-tuple-element.39), channel_id=1, source_target_pairs={{0,128},{1,129},{2,130},{3,131},{4,132},{5,133},{6,134},{7,135},{8... | collective-permute-start | bytes 638984 | tf_op jit(solution)/shard_map/ppermute | solution.py:26
  255.1 31.6 %collective-permute-start.44 = (bf16[128,832]{0,1:T(8,128)(2,1)S(1)}, bf16[128,832]{0,1:T(8,128)(2,1)S(1)}, u32[]{:S(2)}, u32[]{:S(2)}) collective-permute-start(bf16[128,832]{0,1:T(8,128)(2,1)S(1)} %get-tuple-element.39), channel_id=1, source_target_pairs={{0,192},{1,193},{2,194},{3,195},{4,196},{5,197},{6,198},{7,199},{8... | collective-permute-start | bytes 638984 | tf_op jit(solution)/shard_map/ppermute | solution.py:26
  270.0 23.0 %collective-permute-start.71 = (bf16[128,832]{0,1:T(8,128)(2,1)S(1)}, bf16[128,832]{0,1:T(8,128)(2,1)S(1)}, u32[]{:S(2)}, u32[]{:S(2)}) collective-permute-start(bf16[128,832]{0,1:T(8,128)(2,1)S(1)} %get-tuple-element.9), channel_id=1, source_target_pairs={{0,192},{1,193},{2,194},{3,195},{4,196},{5,197},{6,198},{7,199},{8... | collective-permute-start | bytes 638984 | tf_op jit(solution)/shard_map/ppermute | solution.py:26
  289.6 34.6 %collective-permute-start.57 = (bf16[128,1024]{1,0:T(8,128)(2,1)S(1)}, bf16[128,1024]{1,0:T(8,128)(2,1)S(1)}, u32[]{:S(2)}, u32[]{:S(2)}) collective-permute-start(bf16[128,1024]{1,0:T(8,128)(2,1)S(1)} %pad_maximum_fusion.5), channel_id=1, source_target_pairs={{0,6},{1,7},{2,0},{3,1},{4,2},{5,3},{6,4},{7,5},{8,14},{9,15},{10,... | collective-permute-start | bytes 786440 | tf_op jit(solution)/shard_map/ppermute | solution.py:26
  292.3 18.0 %collective-permute-start.50 = (bf16[128,1024]{1,0:T(8,128)(2,1)S(1)}, bf16[128,1024]{1,0:T(8,128)(2,1)S(1)}, u32[]{:S(2)}, u32[]{:S(2)}) collective-permute-start(bf16[128,1024]{1,0:T(8,128)(2,1)S(1)} %get-tuple-element.16), channel_id=1, source_target_pairs={{0,0},{1,1},{2,2},{3,3},{4,4},{5,5},{6,6},{7,7},{8,8},{9,9},{10,10... | collective-permute-start | bytes 786440 | tf_op jit(solution)/shard_map/ppermute | solution.py:26
  293.0 17.3 %collective-permute-start.53 = (bf16[128,1024]{1,0:T(8,128)(2,1)S(1)}, bf16[128,1024]{1,0:T(8,128)(2,1)S(1)}, u32[]{:S(2)}, u32[]{:S(2)}) collective-permute-start(bf16[128,1024]{1,0:T(8,128)(2,1)S(1)} %get-tuple-element.17), channel_id=1, source_target_pairs={{0,8},{1,9},{2,10},{3,11},{4,12},{5,13},{6,14},{7,15},{8,16},{9,17... | collective-permute-start | bytes 786440 | tf_op jit(solution)/shard_map/ppermute | solution.py:26
  299.8 22.5 %collective-permute-start.52 = (bf16[128,1024]{1,0:T(8,128)(2,1)S(1)}, bf16[128,1024]{1,0:T(8,128)(2,1)S(1)}, u32[]{:S(2)}, u32[]{:S(2)}) collective-permute-start(bf16[128,1024]{1,0:T(8,128)(2,1)S(1)} %get-tuple-element.18), channel_id=1, source_target_pairs={{0,16},{1,17},{2,18},{3,19},{4,20},{5,21},{6,22},{7,23},{8,24},{9,... | collective-permute-start | bytes 786440 | tf_op jit(solution)/shard_map/ppermute | solution.py:26
  304.4 17.8 %collective-permute-start.51 = (bf16[128,1024]{1,0:T(8,128)(2,1)S(1)}, bf16[128,1024]{1,0:T(8,128)(2,1)S(1)}, u32[]{:S(2)}, u32[]{:S(2)}) collective-permute-start(bf16[128,1024]{1,0:T(8,128)(2,1)S(1)} %get-tuple-element.19), channel_id=1, source_target_pairs={{0,24},{1,25},{2,26},{3,27},{4,28},{5,29},{6,30},{7,31},{8,0},{9,1... | collective-permute-start | bytes 786440 | tf_op jit(solution)/shard_map/ppermute | solution.py:26
  310.4 16.9 %collective-permute-start.59 = (bf16[128,1024]{1,0:T(8,128)(2,1)S(1)}, bf16[128,1024]{1,0:T(8,128)(2,1)S(1)}, u32[]{:S(2)}, u32[]{:S(2)}) collective-permute-start(bf16[128,1024]{1,0:T(8,128)(2,1)S(1)} %pad_maximum_fusion.7), channel_id=1, source_target_pairs={{0,2},{1,3},{2,4},{3,5},{4,6},{5,7},{6,0},{7,1},{8,10},{9,11},{10,... | collective-permute-start | bytes 786440 | tf_op jit(solution)/shard_map/ppermute | solution.py:26
  322.3 51.0 %collective-permute-start.70 = (bf16[512,832]{0,1:T(8,128)(2,1)S(1)}, bf16[512,832]{0,1:T(8,128)(2,1)S(1)}, u32[]{:S(2)}, u32[]{:S(2)}) collective-permute-start(bf16[512,832]{0,1:T(8,128)(2,1)S(1)} %pad_maximum_fusion.1), channel_id=1, source_target_pairs={{0,32},{1,33},{2,34},{3,35},{4,36},{5,37},{6,38},{7,39},{8,40},{9,... | collective-permute-start | bytes 2555912 | tf_op jit(solution)/shard_map/ppermute | solution.py:26
  338.5 35.8 %collective-permute-start.69 = (bf16[512,832]{0,1:T(8,128)(2,1)S(1)}, bf16[512,832]{0,1:T(8,128)(2,1)}, u32[]{:S(2)}, u32[]{:S(2)}) collective-permute-start(bf16[512,832]{0,1:T(8,128)(2,1)S(1)} %pad_maximum_fusion), channel_id=1, source_target_pairs={{0,32},{1,33},{2,34},{3,35},{4,36},{5,37},{6,38},{7,39},{8,40},{9,... | collective-permute-start | bytes 2555912 | tf_op jit(solution)/shard_map/ppermute | solution.py:26
  338.6 45.6 %collective-permute-start.74 = (bf16[512,832]{0,1:T(8,128)(2,1)S(1)}, bf16[512,832]{0,1:T(8,128)(2,1)}, u32[]{:S(2)}, u32[]{:S(2)}) collective-permute-start(bf16[512,832]{0,1:T(8,128)(2,1)S(1)} %pad_maximum_fusion.2), channel_id=1, source_target_pairs={{0,32},{1,33},{2,34},{3,35},{4,36},{5,37},{6,38},{7,39},{8,40},{9,... | collective-permute-start | bytes 2555912 | tf_op jit(solution)/shard_map/ppermute | solution.py:26
  341.8 17.3 %collective-permute-start.64 = (f32[16,2048]{1,0:T(8,128)S(1)}, f32[16,2048]{1,0:T(8,128)S(1)}, u32[]{:S(2)}, u32[]{:S(2)}) collective-permute-start(f32[16,2048]{1,0:T(8,128)S(1)} %pad_maximum_fusion.8), channel_id=1, source_target_pairs={{0,1},{1,0},{2,3},{3,2},{4,5},{5,4},{6,7},{7,6},{8,9},{9,8},{10,11... | collective-permute-start | bytes 393224 | tf_op jit(solution)/shard_map/ppermute | solution.py:26
  (61 other events, 567.3 us)
